TPU v7x, 32 devices: a whole 2x2x4 slice. The times are simulated.
32 devices in a mesh: lat: 4 (over y, x), ang: 8 (over z, core).
Axes of the slice: x: 2, y: 2, z: 4, core: 2. Of those that a mesh axis runs over, the one named last changes fastest.
Arguments:
- incident: float32 [2, 256, 131072], P(None, 'ang', 'lat'), may hold values from -6 to 6
- detuning: float32 [256], P('ang'), may hold values from -1.5 to 1.5
- phase_table: int32 [3, 131072], P(None, 'lat'), may hold values from -32768 to 32767
- response: float32 [256, 256], replicated, may hold values from 0 to 2, as said below
- counts: int32 [256, 131072], P(None, ('lat', 'ang')), may hold values from 0 to 3
Outputs:
- exit_field: float32 [2, 256, 131072], P(None, 'ang', 'lat')
- estimate: float32 [256, 131072], P('ang', 'lat')
Inputs may be any that keep to these rules, and one draw needn't show every extreme that they name: `response`: every entry is positive.
All inputs are finite; a program needn't handle non-finite values.
Results may differ from a plain program's by a relative error of at most 0.00013.
Values sent between devices are 32-bit elements; how exact they have to be, the bound alone decides.
A program may use at most 128 MiB of HBM per device.

v0:
```python
import functools
import math

import jax
import jax.numpy as jnp
from jax import lax
from jax.experimental import pallas as pl
from jax.experimental.pallas import tpu as pltpu
from jax.sharding import PartitionSpec as P

COLS = 512
BLOCKS = 3
STEPS = 3
ITERS = 6
TOTAL = BLOCKS * STEPS
BEFORE = TOTAL - 2
AFTER = TOTAL
GROUP = 8

coupling = 0.6
background = 0.25
phase_unit = math.pi / 32768.0
tan_kappa = math.tan(coupling)
tan_squared = tan_kappa * tan_kappa
end_scale = math.cos(coupling) ** TOTAL / tan_kappa


def passed_along(x, axis, by):
    devices = lax.axis_size(axis)
    return lax.ppermute(x, axis, [(i, (i + by) % devices) for i in range(devices)])


def table_of(step):
    block, last = divmod(step, STEPS)
    return block + (BLOCKS if last == STEPS - 1 else 0)


def sweep_kernel(halves, dests, *refs):
    (inc, before, after, tab_cos, tab_sin, det_cos, det_sin) = refs[:7]
    exit_ref, *int_refs = refs[-5 - halves : -4]
    beam_re, beam_im, bragg_re, bragg_im = refs[-4:]
    span_rows = inc.shape[2] // COLS
    rows = span_rows + BEFORE + AFTER
    dcos = jnp.broadcast_to(det_cos[...], (GROUP, COLS))
    dsin = jnp.broadcast_to(det_sin[...], (GROUP, COLS))

    def at(k):
        return pl.ds(pl.multiple_of(k * COLS, COLS), COLS)

    def turned(re, im, table, row):
        pc = tab_cos[table, pl.ds(row, 1), :]
        ps = tab_sin[table, pl.ds(row, 1), :]
        a = dcos * re + dsin * im
        b = dcos * im - dsin * re
        return pc * a - ps * b, pc * b + ps * a

    def enter(source, count, shift):
        @pl.loop(0, count)
        def _(k):
            re = source[0, :, at(k)]
            im = source[1, :, at(k)]
            beam_re[:, at(k + shift)] = re
            beam_im[:, at(k + shift)] = im
            out_re, out_im = turned(-tan_squared * im, tan_squared * re, table_of(0), k + shift)
            bragg_re[:, at(k + shift)] = out_re
            bragg_im[:, at(k + shift)] = out_im

    enter(before, BEFORE, 0)
    enter(inc, span_rows, BEFORE)
    enter(after, AFTER, BEFORE + span_rows)

    for step in range(1, TOTAL - 1):

        @pl.loop(0, rows // 2 - step)
        def _(pair):
            for odd in range(2):
                k = pair * 2 + odd
                here, there = at(k), at(k + 2 * step)
                t_re, t_im = beam_re[:, here], beam_im[:, here]
                d_re, d_im = bragg_re[:, there], bragg_im[:, there]
                beam_re[:, here] = t_re - d_im
                beam_im[:, here] = t_im + d_re
                out_re, out_im = turned(
                    d_re - tan_squared * t_im, d_im + tan_squared * t_re, table_of(step), k + step
                )
                bragg_re[:, there] = out_re
                bragg_im[:, there] = out_im

    step = TOTAL - 1
    per_dest = span_rows // dests
    per_half = per_dest // halves

    @pl.loop(0, dests)
    def _(dest):
        for inner in range(per_dest):
            k = dest * per_dest + inner
            here, there = at(k), at(k + 2 * step)
            t_re, t_im = beam_re[:, here], beam_im[:, here]
            d_re, d_im = bragg_re[:, there], bragg_im[:, there]
            out_re, out_im = turned(
                d_re - tan_squared * t_im, d_im + tan_squared * t_re, table_of(step), k + step
            )
            exit_ref[0, :, here] = out_re
            exit_ref[1, :, here] = out_im
            half, place = divmod(inner, per_half)
            int_refs[half][dest, :, place * COLS : (place + 1) * COLS] = out_re * out_re + out_im * out_im


def sweep(group, halo, first, halves, dests, count, incident, tables, detune, exit_field, made):
    _, angles, span = incident.shape
    before, after = halo
    rows = span // COLS + BEFORE + AFTER
    points = span // dests // halves
    place = 0 if made is None else made[0]
    whole = lambda x: pl.BlockSpec(x.shape, lambda i: (0,) * x.ndim)
    in_specs = [
        pl.BlockSpec((2, GROUP, span), lambda i: (0, group, 0)),
        pl.BlockSpec((2, GROUP, before.shape[2]), lambda i: (0, group - first, 0)),
        pl.BlockSpec((2, GROUP, after.shape[2]), lambda i: (0, group - first, 0)),
        whole(tables[0]),
        whole(tables[1]),
        pl.BlockSpec((GROUP, 1), lambda i: (group, 0)),
        pl.BlockSpec((GROUP, 1), lambda i: (group, 0)),
    ]
    operands = [incident, before, after, *tables, *detune]
    aliases = {}
    kept = ([] if exit_field is None else [(0, exit_field)]) + (
        [] if made is None else [(1 + half, x) for half, x in enumerate(made[1])]
    )
    for out, x in kept:
        aliases[len(operands)] = out
        in_specs.append(pl.BlockSpec(memory_space=pl.ANY))
        operands.append(x)
    exit_field, *made = pl.pallas_call(
        functools.partial(sweep_kernel, halves, dests),
        grid=(1,),
        out_shape=[jax.ShapeDtypeStruct((2, angles, span), jnp.float32)]
        + [jax.ShapeDtypeStruct((dests, count * GROUP, points), jnp.float32)] * halves,
        in_specs=in_specs,
        out_specs=[pl.BlockSpec((2, GROUP, span), lambda i: (0, group, 0))]
        + [pl.BlockSpec((dests, GROUP, points), lambda i: (0, place, 0))] * halves,
        scratch_shapes=[pltpu.VMEM((GROUP, rows * COLS), jnp.float32)] * 4,
        input_output_aliases=aliases,
        compiler_params=pltpu.CompilerParams(vmem_limit_bytes=40 * 1024 * 1024),
        cost_estimate=pl.CostEstimate(
            flops=20 * TOTAL * GROUP * rows * COLS,
            bytes_accessed=20 * GROUP * span,
            transcendentals=0,
        ),
    )(*operands)
    return exit_field, (place + 1, made)


def place_kernel(source, *refs):
    refs[-1][...] = source[0]


def placed(half, halves, x, whole):
    dests, angles, part = x.shape
    kept = [] if whole is None else [whole]
    return pl.pallas_call(
        place_kernel,
        grid=(dests,),
        out_shape=jax.ShapeDtypeStruct((angles, dests * halves * part), jnp.float32),
        in_specs=[pl.BlockSpec((1, angles, part), lambda i: (i, 0, 0))]
        + [pl.BlockSpec(memory_space=pl.ANY)] * len(kept),
        out_specs=pl.BlockSpec((angles, part), lambda i: (0, i * halves + half)),
        input_output_aliases={1: 0} if kept else {},
        cost_estimate=pl.CostEstimate(flops=0, bytes_accessed=8 * x.size, transcendentals=0),
    )(x, *kept)


def phase_tables(phase):
    earlier = jnp.roll(phase, 1, axis=1)
    leaving = jnp.concatenate([earlier[1:], jnp.zeros_like(phase[:1])], axis=0)
    turns = jnp.concatenate([phase - earlier, phase - leaving], axis=0)
    angle = turns * phase_unit
    scale = jnp.ones((2 * BLOCKS, 1, 1), jnp.float32).at[2 * BLOCKS - 1].set(end_scale)
    return jnp.cos(angle) * scale, jnp.sin(angle) * scale


def deconvolve(response, backward, estimate, counts):
    measured = counts.astype(jnp.float32)
    for _ in range(ITERS):
        blurred = (
            jnp.dot(
                response,
                estimate,
                precision=lax.Precision.HIGH,
                preferred_element_type=jnp.float32,
            )
            + background
        )
        projected = lax.dot_general(
            backward,
            measured / blurred,
            (((0,), (0,)), ((), ())),
            precision=lax.Precision.HIGH,
            preferred_element_type=jnp.float32,
        )
        estimate = estimate * projected
    return estimate


def on_device(incident, detuning, phase_table, response, counts):
    _, angles, span = incident.shape
    dests = lax.axis_size("ang")
    points = span // dests
    halves = 2 if (points // COLS) % 2 == 0 else 1
    part = points // halves
    groups = angles // GROUP

    def neighbours(x):
        return (
            passed_along(x[..., span - BEFORE * COLS :], "lat", 1),
            passed_along(x[..., : AFTER * COLS], "lat", -1),
        )

    def exchanged(x):
        return lax.all_to_all(x, "ang", split_axis=0, concat_axis=0, tiled=True)

    phase = phase_table.astype(jnp.float32)
    ends = (slice(span - BEFORE * COLS, span), slice(0, AFTER * COLS))
    before, after = (
        passed_along(
            jnp.concatenate([incident[0, :GROUP, end], incident[1, :GROUP, end], phase[:, end]]), "lat", by
        )
        for end, by in zip(ends, (1, -1))
    )
    phase = jnp.concatenate([before[2 * GROUP :], phase, after[2 * GROUP :]], axis=1)
    tables = phase_tables(phase.reshape(BLOCKS, -1, COLS))
    halos = {0: (0, tuple(x[: 2 * GROUP].reshape(2, GROUP, -1) for x in (before, after)))}
    group = 1
    while group < groups:
        count = 1 if group == 1 else groups - group
        halo = neighbours(incident[:, group * GROUP : (group + count) * GROUP])
        for one in range(group, group + count):
            halos[one] = (group, halo)
        group += count
    detune = (jnp.cos(detuning)[:, None], jnp.sin(detuning)[:, None])

    exit_field, (_, made) = sweep(
        0, halos[0][1], 0, 1, dests, 1, incident, tables, detune, None, None
    )
    early = exchanged(made[0])
    late = []
    if groups > 1:
        made = None
        for group in range(1, groups):
            first, halo = halos[group]
            exit_field, made = sweep(
                group, halo, first, halves, dests, groups - 1, incident, tables, detune, exit_field, made
            )
        for half in range(halves):
            late.append(exchanged(made[1][half]))
    backward = response / jnp.sum(response, axis=0)[None, :]
    whole = None
    for half in range(halves):
        start = jnp.concatenate(
            [early[:, :, half * part : (half + 1) * part]] + late[half : half + 1], axis=1
        )
        early, start = lax.optimization_barrier((early, start))
        estimate = deconvolve(
            response,
            backward,
            start.reshape(dests * angles, part),
            counts[:, half * part : (half + 1) * part],
        )
        whole = placed(half, halves, exchanged(estimate.reshape(dests, angles, part)), whole)
    return (exit_field, whole)


def solution(mesh):
    return jax.shard_map(
        on_device,
        mesh=mesh,
        in_specs=(P(None, "ang", "lat"), P("ang"), P(None, "lat"), P(), P(None, ("lat", "ang"))),
        out_specs=(P(None, "ang", "lat"), P("ang", "lat")),
        check_vma=False,
    )
```

profile of v0, /device:TPU:0, one launch (start us, length us, event | category | flops | bytes accessed | tf_op | source)
XLA Modules:
  0.0 317.1 jit_solution(16717631709104800415)
XLA Ops:
  2.8 3.0 collective-permute-start.2
  8.1 7.5 %collective-permute-done.2 = f32[19,3584]{1,0:T(8,128)S(1)} collective-permute-done((f32[19,3584]{1,0:T(8,128)S(1)}, f32[19,3584]{1,0:T(8,128)S(1)}, u32[]{:S(2)}, u32[]{:S(2)}) %collective-permute-start.2) | collective-permute-done | bytes 272416 | tf_op jit(solution)/shard_map/ppermute | solution.py:30
  15.7 8.9 %collective-permute-done.3 = f32[19,4608]{1,0:T(8,128)S(1)} collective-permute-done((f32[19,4608]{1,0:T(8,128)S(1)}, f32[19,4608]{1,0:T(8,128)S(1)}, u32[]{:S(2)}, u32[]{:S(2)}) %collective-permute-start.3) | collective-permute-done | bytes 350240 | tf_op jit(solution)/shard_map/ppermute | solution.py:30
  25.2 3.7 %sine_multiply_fusion = (f32[6,80,512]{2,1,0:T(8,128)S(1)}, f32[6,80,512]{2,1,0:T(8,128)S(1)}) fusion(f32[3,80,512]{2,1,0:T(8,128)S(1)} %get-tuple-element.49, f32[3,80,512]{2,1,0:T(8,128)S(1)} %get-tuple-element.48, f32[6]{0:T(128)S(1)} %copy-done.5), kind=kLoop, calls=%fused_computation.51 | loop fusion | flops 983040 | bytes 2949144 | tf_op jit(solution)/shard_map/mul | solution.py:179
  28.9 10.9 %shard_map.68 = (f32[2,32,32768]{2,1,0:T(8,128)}, f32[8,8,4096]{2,1,0:T(8,128)}) custom-call(f32[2,32,32768]{2,1,0:T(8,128)S(1)} %copy-done, f32[2,8,3584]{2,1,0:T(8,128)S(1)} %slice_bitcast_fusion.1.refs_1_, f32[2,8,4608]{2,1,0:T(8,128)S(1)} %slice_bitcast_fusion.refs_2_, f32[6,80,512]{2,1,0:T(8,128)S(1)} %get-tuple-element.47.refs_3_, ...), custom_call_target="tpu_custom_call" | custom-call | flops 58982400 | bytes 5242880 | tf_op jit(solution)/shard_map/pallas_call | solution.py:134
  39.9 4.9 %all-to-all-start = ((f32[8,8,4096]{2,1,0:T(8,128)}), f32[8,8,4096]{2,1,0:T(8,128)S(1)}, u32[]{:S(2)}, u32[]{:S(2)}) async-start(f32[8,8,4096]{2,1,0:T(8,128)} %get-tuple-element.36), calls=%async_computation | async-start | bytes 2097152 | tf_op jit(solution)/shard_map/all_to_all | solution.py:220
  50.0 2.4 collective-permute-start.5
  53.5 29.2 %collective-permute-done.4.refs_1_ = f32[2,8,3584]{2,1,0:T(8,128)S(1)} collective-permute-done((f32[2,8,3584]{2,1,0:T(8,128)S(1)}, f32[2,8,3584]{2,1,0:T(8,128)S(1)}, u32[]{:S(2)}, u32[]{:S(2)}) %collective-permute-start.4) | collective-permute-done | bytes 229408 | tf_op jit(solution)/shard_map/ppermute | solution.py:30
  82.7 3.4 %copy-done.1 = f32[2,32,32768]{2,1,0:T(8,128)S(1)} copy-done((f32[2,32,32768]{2,1,0:T(8,128)S(1)}, f32[2,32,32768]{2,1,0:T(8,128)}, u32[]{:S(2)}) %copy-start.1) | copy-done | bytes 8388632
  86.1 10.9 %shard_map.69 = (f32[2,32,32768]{2,1,0:T(8,128)}, f32[8,24,2048]{2,1,0:T(8,128)}, f32[8,24,2048]{2,1,0:T(8,128)}) custom-call(f32[2,32,32768]{2,1,0:T(8,128)S(1)} %copy-done.1, f32[2,8,3584]{2,1,0:T(8,128)S(1)} %collective-permute-done.4.refs_1_, f32[2,8,4608]{2,1,0:T(8,128)S(1)} %collective-permute-done.5.refs_2_, ...), custom_call_target="tpu_custom_call", output_to_operand_aliasing={{0}: (7, {})} | custom-call | flops 58982400 | bytes 5242880 | tf_op jit(solution)/shard_map/pallas_call | solution.py:134
  97.0 11.0 %shard_map.70 = (f32[2,32,32768]{2,1,0:T(8,128)}, f32[8,24,2048]{2,1,0:T(8,128)}, f32[8,24,2048]{2,1,0:T(8,128)}) custom-call(f32[2,32,32768]{2,1,0:T(8,128)S(1)} %copy-done.1, f32[2,16,3584]{2,1,0:T(8,128)S(1)} %collective-permute-done.refs_1_, ...), custom_call_target="tpu_custom_call", output_to_operand_aliasing={{0}: (7, {}), {1}: (8, {}), {2}: (9, {})} | custom-call | flops 58982400 | bytes 5242880 | tf_op jit(solution)/shard_map/pallas_call | solution.py:134
  108.0 11.0 %shard_map.71 = (f32[2,32,32768]{2,1,0:T(8,128)}, f32[8,24,2048]{2,1,0:T(8,128)}, f32[8,24,2048]{2,1,0:T(8,128)}) custom-call(f32[2,32,32768]{2,1,0:T(8,128)S(1)} %copy-done.1, f32[2,16,3584]{2,1,0:T(8,128)S(1)} %collective-permute-done.refs_1_, ...), custom_call_target="tpu_custom_call", output_to_operand_aliasing={{0}: (7, {}), {1}: (8, {}), {2}: (9, {})} | custom-call | flops 58982400 | bytes 5242880 | tf_op jit(solution)/shard_map/pallas_call | solution.py:134
  118.9 4.9 %all-to-all-start.1 = ((f32[8,24,2048]{2,1,0:T(8,128)}), f32[8,24,2048]{2,1,0:T(8,128)S(1)}, u32[]{:S(2)}, u32[]{:S(2)}) async-start(f32[8,24,2048]{2,1,0:T(8,128)} %get-tuple-element.37), calls=%async_computation.1 | async-start | bytes 3145728 | tf_op jit(solution)/shard_map/all_to_all | solution.py:220
  123.9 37.8 %all-to-all-done.1 = f32[8,24,2048]{2,1,0:T(8,128)S(1)} async-done(((f32[8,24,2048]{2,1,0:T(8,128)}), f32[8,24,2048]{2,1,0:T(8,128)S(1)}, u32[]{:S(2)}, u32[]{:S(2)}) %all-to-all-start.1) | async-done | bytes 1572896 | tf_op jit(solution)/shard_map/all_to_all | solution.py:220
  161.7 4.6 %all-to-all-start.2 = ((f32[8,24,2048]{2,1,0:T(8,128)}), f32[8,24,2048]{2,1,0:T(8,128)}, u32[]{:S(2)}, u32[]{:S(2)}) async-start(f32[8,24,2048]{2,1,0:T(8,128)} %get-tuple-element.39), calls=%async_computation.2 | async-start | bytes 3145728 | tf_op jit(solution)/shard_map/all_to_all | solution.py:220
  182.8 2.6 convolution_multiply_fusion
  185.4 18.5 %all-to-all-done.2 = f32[8,24,2048]{2,1,0:T(8,128)} async-done(((f32[8,24,2048]{2,1,0:T(8,128)}), f32[8,24,2048]{2,1,0:T(8,128)}, u32[]{:S(2)}, u32[]{:S(2)}) %all-to-all-start.2) | async-done | bytes 1572896 | tf_op jit(solution)/shard_map/all_to_all | solution.py:220
  203.9 3.7 %all-to-all-start.4 = ((f32[8,32,2048]{2,1,0:T(8,128)}), f32[8,32,2048]{2,1,0:T(8,128)S(1)}, u32[]{:S(2)}, u32[]{:S(2)}) async-start(f32[8,32,2048]{2,1,0:T(8,128)} %bitcast.111), calls=%async_computation.4 | async-start | bytes 4194304 | tf_op jit(solution)/shard_map/all_to_all | solution.py:220
  224.7 2.6 convolution_multiply_fusion.6
  227.3 29.3 %all-to-all-done.4.source = f32[8,32,2048]{2,1,0:T(8,128)S(1)} async-done(((f32[8,32,2048]{2,1,0:T(8,128)}), f32[8,32,2048]{2,1,0:T(8,128)S(1)}, u32[]{:S(2)}, u32[]{:S(2)}) %all-to-all-start.4) | async-done | bytes 2097184 | tf_op jit(solution)/shard_map/all_to_all | solution.py:220
  258.0 4.3 %all-to-all-start.3 = ((f32[8,32,2048]{2,1,0:T(8,128)}), f32[8,32,2048]{2,1,0:T(8,128)}, u32[]{:S(2)}, u32[]{:S(2)}) async-start(f32[8,32,2048]{2,1,0:T(8,128)} %bitcast.112), calls=%async_computation.3 | async-start | bytes 4194304 | tf_op jit(solution)/shard_map/all_to_all | solution.py:220
  262.4 5.6 %shard_map.72.refs_0_ = f32[32,32768]{1,0:T(8,128)} custom-call(f32[8,32,2048]{2,1,0:T(8,128)} %copy-done.3), custom_call_target="tpu_custom_call" | custom-call | bytes 4194304 | tf_op jit(solution)/shard_map/pallas_call | solution.py:161
  268.0 43.4 %all-to-all-done.3.source = f32[8,32,2048]{2,1,0:T(8,128)} async-done(((f32[8,32,2048]{2,1,0:T(8,128)}), f32[8,32,2048]{2,1,0:T(8,128)}, u32[]{:S(2)}, u32[]{:S(2)}) %all-to-all-start.3) | async-done | bytes 2097184 | tf_op jit(solution)/shard_map/all_to_all | solution.py:220
  311.4 5.6 %shard_map.73 = f32[32,32768]{1,0:T(8,128)} custom-call(f32[8,32,2048]{2,1,0:T(8,128)} %all-to-all-done.3.source, f32[32,32768]{1,0:T(8,128)} %shard_map.72.refs_0_), custom_call_target="tpu_custom_call", output_to_operand_aliasing={{}: (1, {})} | custom-call | bytes 4194304 | tf_op jit(solution)/shard_map/pallas_call | solution.py:161
  (77 shorter events, 46.2 us)
Async XLA Ops:
  0.6 7.3 %copy-start.8 = (f32[32]{0:T(128)S(1)}, f32[32]{0:T(128)}, u32[]{:S(2)}) copy-start(f32[32]{0:T(128)} %param.8) | copy-start | bytes 388
  2.8 12.8 %collective-permute-start.2 = (f32[19,3584]{1,0:T(8,128)S(1)}, f32[19,3584]{1,0:T(8,128)S(1)}, u32[]{:S(2)}, u32[]{:S(2)}) collective-permute-start(f32[19,3584]{1,0:T(8,128)S(1)} %pad_maximum_fusion.5), channel_id=1, source_target_pairs={{0,8},{8,16},{16,24},{24,0},{1,9},{9,17},{17,25},{25,1},{2,10},{10... | collective-permute-start | bytes 817160 | tf_op jit(solution)/shard_map/ppermute | solution.py:30
  6.9 17.7 %collective-permute-start.3 = (f32[19,4608]{1,0:T(8,128)S(1)}, f32[19,4608]{1,0:T(8,128)S(1)}, u32[]{:S(2)}, u32[]{:S(2)}) collective-permute-start(f32[19,4608]{1,0:T(8,128)S(1)} %pad_maximum_fusion.4), channel_id=1, source_target_pairs={{0,24},{8,0},{16,8},{24,16},{1,25},{9,1},{17,9},{25,17},{2,26},{10... | collective-permute-start | bytes 1050632 | tf_op jit(solution)/shard_map/ppermute | solution.py:30
  24.5 0.7 copy-start.5
  24.6 4.4 %copy-start = (f32[2,32,32768]{2,1,0:T(8,128)S(1)}, f32[2,32,32768]{2,1,0:T(8,128)}, u32[]{:S(2)}) copy-start(f32[2,32,32768]{2,1,0:T(8,128)} %refs_0_.7) | copy-start | bytes 25165828
  39.9 79.1 %all-to-all-start = ((f32[8,8,4096]{2,1,0:T(8,128)}), f32[8,8,4096]{2,1,0:T(8,128)S(1)}, u32[]{:S(2)}, u32[]{:S(2)}) async-start(f32[8,8,4096]{2,1,0:T(8,128)} %get-tuple-element.36), calls=%async_computation | async-start | bytes 2097152 | tf_op jit(solution)/shard_map/all_to_all | solution.py:220
  45.9 51.1 %collective-permute-start.1 = (f32[2,16,4608]{2,1,0:T(8,128)S(1)}, f32[2,16,4608]{2,1,0:T(8,128)S(1)}, u32[]{:S(2)}, u32[]{:S(2)}) collective-permute-start(f32[2,16,4608]{2,1,0:T(8,128)S(1)} %slice.91), channel_id=1, source_target_pairs={{0,24},{8,0},{16,8},{24,16},{1,25},{9,1},{17,9},{25,17},{2,26},{10... | collective-permute-start | bytes 1769480 | tf_op jit(solution)/shard_map/ppermute | solution.py:30
  48.4 48.6 %collective-permute-start = (f32[2,16,3584]{2,1,0:T(8,128)S(1)}, f32[2,16,3584]{2,1,0:T(8,128)S(1)}, u32[]{:S(2)}, u32[]{:S(2)}) collective-permute-start(f32[2,16,3584]{2,1,0:T(8,128)S(1)} %slice.90), channel_id=1, source_target_pairs={{0,8},{8,16},{16,24},{24,0},{1,9},{9,17},{17,25},{25,1},{2,10},{10... | collective-permute-start | bytes 1376264 | tf_op jit(solution)/shard_map/ppermute | solution.py:30
  50.0 32.6 %collective-permute-start.5 = (f32[2,8,4608]{2,1,0:T(8,128)S(1)}, f32[2,8,4608]{2,1,0:T(8,128)S(1)}, u32[]{:S(2)}, u32[]{:S(2)}) collective-permute-start(f32[2,8,4608]{2,1,0:T(8,128)S(1)} %slice.104), channel_id=1, source_target_pairs={{0,24},{8,0},{16,8},{24,16},{1,25},{9,1},{17,9},{25,17},{2,26},{10... | collective-permute-start | bytes 884744 | tf_op jit(solution)/shard_map/ppermute | solution.py:30
  53.4 29.3 %collective-permute-start.4 = (f32[2,8,3584]{2,1,0:T(8,128)S(1)}, f32[2,8,3584]{2,1,0:T(8,128)S(1)}, u32[]{:S(2)}, u32[]{:S(2)}) collective-permute-start(f32[2,8,3584]{2,1,0:T(8,128)S(1)} %slice.103), channel_id=1, source_target_pairs={{0,8},{8,16},{16,24},{24,0},{1,9},{9,17},{17,25},{25,1},{2,10},{10... | collective-permute-start | bytes 688136 | tf_op jit(solution)/shard_map/ppermute | solution.py:30
  82.7 3.4 %copy-start.1 = (f32[2,32,32768]{2,1,0:T(8,128)S(1)}, f32[2,32,32768]{2,1,0:T(8,128)}, u32[]{:S(2)}) copy-start(f32[2,32,32768]{2,1,0:T(8,128)} %refs_0_.7) | copy-start | bytes 25165828
  118.9 4.9 %copy-start.2 = (f32[256,256]{1,0:T(8,128)S(1)}, f32[256,256]{1,0:T(8,128)}, u32[]{:S(2)}) copy-start(f32[256,256]{1,0:T(8,128)} %param.10) | copy-start | bytes 786436
  118.9 4.9 %copy-start.4 = (f32[8,8,4096]{2,1,0:T(8,128)}, f32[8,8,4096]{2,1,0:T(8,128)S(1)}, u32[]{:S(2)}) copy-start(f32[8,8,4096]{2,1,0:T(8,128)S(1)} %all-to-all-done) | copy-start | bytes 3145732
  118.9 42.7 %all-to-all-start.1 = ((f32[8,24,2048]{2,1,0:T(8,128)}), f32[8,24,2048]{2,1,0:T(8,128)S(1)}, u32[]{:S(2)}, u32[]{:S(2)}) async-start(f32[8,24,2048]{2,1,0:T(8,128)} %get-tuple-element.37), calls=%async_computation.1 | async-start | bytes 3145728 | tf_op jit(solution)/shard_map/all_to_all | solution.py:220
  161.7 4.6 %slice-start = ((f32[8,8,4096]{2,1,0:T(8,128)}), f32[8,8,2048]{2,1,0:T(8,128)S(1)}, s32[]{:S(2)}) async-start(f32[8,8,4096]{2,1,0:T(8,128)} %copy-done.4), calls=%async_computation.5 | async-start | bytes 1048576 | tf_op jit(solution)/shard_map/slice | solution.py:260
  161.7 42.3 %all-to-all-start.2 = ((f32[8,24,2048]{2,1,0:T(8,128)}), f32[8,24,2048]{2,1,0:T(8,128)}, u32[]{:S(2)}, u32[]{:S(2)}) async-start(f32[8,24,2048]{2,1,0:T(8,128)} %get-tuple-element.39), calls=%async_computation.2 | async-start | bytes 3145728 | tf_op jit(solution)/shard_map/all_to_all | solution.py:220
  166.3 2.2 copy-start.6
  203.9 3.7 %slice-start.1 = ((f32[8,8,4096]{2,1,0:T(8,128)}), f32[8,8,2048]{2,1,0:T(8,128)S(1)}, s32[]{:S(2)}) async-start(f32[8,8,4096]{2,1,0:T(8,128)} %copy-done.4), calls=%async_computation.6 | async-start | bytes 1048576 | tf_op jit(solution)/shard_map/slice | solution.py:260
  203.9 52.7 %all-to-all-start.4 = ((f32[8,32,2048]{2,1,0:T(8,128)}), f32[8,32,2048]{2,1,0:T(8,128)S(1)}, u32[]{:S(2)}, u32[]{:S(2)}) async-start(f32[8,32,2048]{2,1,0:T(8,128)} %bitcast.111), calls=%async_computation.4 | async-start | bytes 4194304 | tf_op jit(solution)/shard_map/all_to_all | solution.py:220
  207.7 2.7 copy-start.7
  256.7 1.4 copy-start.3
  258.0 53.4 %all-to-all-start.3 = ((f32[8,32,2048]{2,1,0:T(8,128)}), f32[8,32,2048]{2,1,0:T(8,128)}, u32[]{:S(2)}, u32[]{:S(2)}) async-start(f32[8,32,2048]{2,1,0:T(8,128)} %bitcast.112), calls=%async_computation.3 | async-start | bytes 4194304 | tf_op jit(solution)/shard_map/all_to_all | solution.py:220
where the time goes:
time: 318 us; the launch traced here: 317 us
  waiting for transfers between devices  175 us (55%)
  Pallas kernels  55.1 us (17%)
  matrix products  33.7 us (11%)
  starting transfers between devices  31.1 us (10%)
  local copies, waits for them, and re-layouts  14.2 us (4%)
  other arithmetic  7.26 us (2%)
    all_to_all x5, waiting for transfers between devices, exchanged(): return lax.all_to_all(x, 'ang', split_axis=0, concat_axis=0, tiled=True)  129 us
    ppermute x6, waiting for transfers between devices, passed_along(): lax.ppermute(x, axis, [(i, (i + by) % devices) for i in range(devices)])  45.6 us
    pallas_call x4, Pallas kernels, sweep(): pl.pallas_call(functools.partial(sweep_kernel, halves, dests), grid=(1,),...  43.8 us
    all_to_all x5, starting transfers between devices, exchanged(): return lax.all_to_all(x, 'ang', split_axis=0, concat_axis=0, tiled=True)  22.4 us
    dot_general x12, matrix products, deconvolve(): lax.dot_general(backward, measured / blurred, (((0,), (0,)), ((), ())), p...  17.7 us
    dot_general x12, matrix products, deconvolve(): jnp.dot(response, estimate, precision=lax.Precision.HIGH, preferred_eleme...  16 us
    pallas_call x2, Pallas kernels, placed(): pl.pallas_call(place_kernel, grid=(dests,), out_shape=jax.ShapeDtypeStruc...  11.3 us
    ppermute x6, starting transfers between devices, passed_along(): lax.ppermute(x, axis, [(i, (i + by) % devices) for i in range(devices)])  8.66 us
  transfers between devices with their start and end apart: 11, of which 7 were waited for; matrix products, arithmetic and copies ran while one was open for 13% of the time, Pallas kernels for 12%

commit v1 on v0

--- a/solution.py
+++ b/solution.py
@@ -144,27 +144,37 @@
         compiler_params=pltpu.CompilerParams(vmem_limit_bytes=40 * 1024 * 1024),
         cost_estimate=pl.CostEstimate(
             flops=20 * TOTAL * GROUP * rows * COLS,
-            bytes_accessed=20 * GROUP * span,
+            bytes_accessed=28 * GROUP * span,
             transcendentals=0,
         ),
     )(*operands)
     return exit_field, (place + 1, made)
 
 
-def place_kernel(source, *refs):
-    refs[-1][...] = source[0]
+def place_kernel(half, halves, source, *refs):
+    whole, sems = refs[-2:]
+    dests, _, part = source.shape
+    copies = [
+        pltpu.make_async_copy(
+            source.at[i], whole.at[:, pl.ds((i * halves + half) * part, part)], sems.at[i]
+        )
+        for i in range(dests)
+    ]
+    for copy in copies:
+        copy.start()
+    for copy in copies:
+        copy.wait()
 
 
 def placed(half, halves, x, whole):
     dests, angles, part = x.shape
     kept = [] if whole is None else [whole]
     return pl.pallas_call(
-        place_kernel,
-        grid=(dests,),
+        functools.partial(place_kernel, half, halves),
         out_shape=jax.ShapeDtypeStruct((angles, dests * halves * part), jnp.float32),
-        in_specs=[pl.BlockSpec((1, angles, part), lambda i: (i, 0, 0))]
-        + [pl.BlockSpec(memory_space=pl.ANY)] * len(kept),
-        out_specs=pl.BlockSpec((angles, part), lambda i: (0, i * halves + half)),
+        in_specs=[pl.BlockSpec(memory_space=pl.ANY)] * (1 + len(kept)),
+        out_specs=pl.BlockSpec(memory_space=pl.ANY),
+        scratch_shapes=[pltpu.SemaphoreType.DMA((dests,))],
         input_output_aliases={1: 0} if kept else {},
         cost_estimate=pl.CostEstimate(flops=0, bytes_accessed=8 * x.size, transcendentals=0),
     )(x, *kept)
@@ -232,24 +242,28 @@
     halos = {0: (0, tuple(x[: 2 * GROUP].reshape(2, GROUP, -1) for x in (before, after)))}
     group = 1
     while group < groups:
-        count = 1 if group == 1 else groups - group
+        count = 1
         halo = neighbours(incident[:, group * GROUP : (group + count) * GROUP])
         for one in range(group, group + count):
             halos[one] = (group, halo)
         group += count
     detune = (jnp.cos(detuning)[:, None], jnp.sin(detuning)[:, None])
 
-    exit_field, (_, made) = sweep(
-        0, halos[0][1], 0, 1, dests, 1, incident, tables, detune, None, None
-    )
-    early = exchanged(made[0])
+    lead = max(groups // 2, 1)
+    exit_field = made = None
+    for group in range(lead):
+        first, halo = halos[group]
+        exit_field, made = sweep(
+            group, halo, first, 1, dests, lead, incident, tables, detune, exit_field, made
+        )
+    early = exchanged(made[1][0])
     late = []
-    if groups > 1:
+    if groups > lead:
         made = None
-        for group in range(1, groups):
+        for group in range(lead, groups):
             first, halo = halos[group]
             exit_field, made = sweep(
-                group, halo, first, halves, dests, groups - 1, incident, tables, detune, exit_field, made
+                group, halo, first, halves, dests, groups - lead, incident, tables, detune, exit_field, made
             )
         for half in range(halves):
             late.append(exchanged(made[1][half]))

time: 318 us -> 361 us (1.14)
  Pallas kernels: 55.1 us -> 172 us
  waiting for transfers between devices: 175 us -> 89.8 us
  local copies, waits for them, and re-layouts: 14.2 us -> 23.9 us
    pallas_call x2, Pallas kernels: 11.3 us -> 129 us  [placed(): pl.pallas_call(functools.partial(place_kernel, half, halves), out_shape=j...]
    all_to_all x5, waiting for transfers between devices: 129 us -> 62.2 us  [exchanged(): return lax.all_to_all(x, 'ang', split_axis=0, concat_axis=0, tiled=True)]
    ppermute x6 -> x8, waiting for transfers between devices: 45.6 us -> 27.6 us  [passed_along(): lax.ppermute(x, axis, [(i, (i + by) % devices) for i in range(devices)])]
    unnamed x19 -> x23, local copies, waits for them, and re-layouts: 7.86 us -> 13 us
    slice x4 -> x2, local copies, waits for them, and re-layouts: 0.01 us -> 3.62 us  [on_device(): early[:, :, half * part:(half + 1) * part]]
    ppermute x6 -> x8, starting transfers between devices: 8.66 us -> 11.9 us  [passed_along(): lax.ppermute(x, axis, [(i, (i + by) % devices) for i in range(devices)])]
  transfers between devices with their start and end apart: 11 -> 13, of which waited for: 7 -> 6; matrix products, arithmetic and copies ran while one was open for 13% -> 14% of each run, Pallas kernels for 12% -> 27%
where the time goes in v1:
time: 361 us
  Pallas kernels  172 us (48%)
  waiting for transfers between devices  89.8 us (25%)
  matrix products  34 us (9%)
  starting transfers between devices  32.2 us (9%)
  local copies, waits for them, and re-layouts  23.9 us (7%)
  other arithmetic  6.99 us (2%)
    pallas_call x2, Pallas kernels, placed(): pl.pallas_call(functools.partial(place_kernel, half, halves), out_shape=j...  129 us
    all_to_all x5, waiting for transfers between devices, exchanged(): return lax.all_to_all(x, 'ang', split_axis=0, concat_axis=0, tiled=True)  62.2 us
    pallas_call x4, Pallas kernels, sweep(): pl.pallas_call(functools.partial(sweep_kernel, halves, dests), grid=(1,),...  43.1 us
    ppermute x8, waiting for transfers between devices, passed_along(): lax.ppermute(x, axis, [(i, (i + by) % devices) for i in range(devices)])  27.6 us
    all_to_all x5, starting transfers between devices, exchanged(): return lax.all_to_all(x, 'ang', split_axis=0, concat_axis=0, tiled=True)  20.3 us
    dot_general x12, matrix products, deconvolve(): lax.dot_general(backward, measured / blurred, (((0,), (0,)), ((), ())), p...  18 us
    dot_general x12, matrix products, deconvolve(): jnp.dot(response, estimate, precision=lax.Precision.HIGH, preferred_eleme...  15.9 us
    unnamed x23, local copies, waits for them, and re-layouts  13 us
  transfers between devices with their start and end apart: 13, of which 6 were waited for; matrix products, arithmetic and copies ran while one was open for 14% of the time, Pallas kernels for 27%

profile of v1, /device:TPU:0, one launch (start us, length us, event | category | flops | bytes accessed | tf_op | source)
XLA Modules:
  0.0 360.6 jit_solution(10796248750762331457)
XLA Ops:
  2.8 3.9 %collective-permute-start.3 = (f32[19,4608]{1,0:T(8,128)S(1)}, f32[19,4608]{1,0:T(8,128)S(1)}, u32[]{:S(2)}, u32[]{:S(2)}) collective-permute-start(f32[19,4608]{1,0:T(8,128)S(1)} %pad_maximum_fusion.4), channel_id=1, source_target_pairs={{0,24},{8,0},{16,8},{24,16},{1,25},{9,1},{17,9},{25,17},{2,26},{10... | collective-permute-start | bytes 1050632 | tf_op jit(solution)/shard_map/ppermute | solution.py:30
  9.1 3.0 collective-permute-start.7
  14.3 11.5 %collective-permute-done.2 = f32[19,3584]{1,0:T(8,128)} collective-permute-done((f32[19,3584]{1,0:T(8,128)S(1)}, f32[19,3584]{1,0:T(8,128)}, u32[]{:S(2)}, u32[]{:S(2)}) %collective-permute-start.2) | collective-permute-done | bytes 272416 | tf_op jit(solution)/shard_map/ppermute | solution.py:30
  28.7 3.7 %sine_multiply_fusion = (f32[6,80,512]{2,1,0:T(8,128)S(1)}, f32[6,80,512]{2,1,0:T(8,128)S(1)}) fusion(f32[3,80,512]{2,1,0:T(8,128)S(1)} %get-tuple-element.53, f32[3,80,512]{2,1,0:T(8,128)S(1)} %get-tuple-element.52, f32[6]{0:T(128)S(1)} %copy-done.7), kind=kLoop, calls=%fused_computation.51 | loop fusion | flops 983040 | bytes 2949144 | tf_op jit(solution)/shard_map/mul | solution.py:189
  32.4 3.4 copy-done
  35.8 10.6 %shard_map.68 = (f32[2,32,32768]{2,1,0:T(8,128)}, f32[8,16,4096]{2,1,0:T(8,128)S(1)}) custom-call(f32[2,32,32768]{2,1,0:T(8,128)S(1)} %copy-done, f32[2,8,3584]{2,1,0:T(8,128)S(1)} %slice_bitcast_fusion.1.refs_1_, f32[2,8,4608]{2,1,0:T(8,128)S(1)} %slice_bitcast_fusion.refs_2_, f32[6,80,512]{2,1,0:T(8,128)S(1)} %get-tuple-element.51.refs_3_, ...), custom_call_target="tpu_custom_call" | custom-call | flops 58982400 | bytes 7340032 | tf_op jit(solution)/shard_map/pallas_call | solution.py:134
  46.4 10.6 %shard_map.69 = (f32[2,32,32768]{2,1,0:T(8,128)}, f32[8,16,4096]{2,1,0:T(8,128)S(1)}) custom-call(f32[2,32,32768]{2,1,0:T(8,128)S(1)} %copy-done, f32[2,8,3584]{2,1,0:T(8,128)S(1)} %collective-permute-done.6.refs_1_, f32[2,8,4608]{2,1,0:T(8,128)S(1)} %collective-permute-done.7.refs_2_, ...), custom_call_target="tpu_custom_call", output_to_operand_aliasing={{0}: (7, {}), {1}: (8, {})} | custom-call | flops 58982400 | bytes 7340032 | tf_op jit(solution)/shard_map/pallas_call | solution.py:134
  58.3 5.0 %all-to-all-start = ((f32[8,16,4096]{2,1,0:T(8,128)}), f32[8,16,4096]{2,1,0:T(8,128)}, u32[]{:S(2)}, u32[]{:S(2)}) async-start(f32[8,16,4096]{2,1,0:T(8,128)} %copy-done.2), calls=%async_computation | async-start | bytes 4194304 | tf_op jit(solution)/shard_map/all_to_all | solution.py:230
  68.2 16.0 %collective-permute-done.4.refs_1_ = f32[2,8,3584]{2,1,0:T(8,128)S(1)} collective-permute-done((f32[2,8,3584]{2,1,0:T(8,128)S(1)}, f32[2,8,3584]{2,1,0:T(8,128)S(1)}, u32[]{:S(2)}, u32[]{:S(2)}) %collective-permute-start.4) | collective-permute-done | bytes 229408 | tf_op jit(solution)/shard_map/ppermute | solution.py:30
  84.3 3.4 copy-done.1
  87.6 10.9 %shard_map.70 = (f32[2,32,32768]{2,1,0:T(8,128)}, f32[8,16,2048]{2,1,0:T(8,128)}, f32[8,16,2048]{2,1,0:T(8,128)}) custom-call(f32[2,32,32768]{2,1,0:T(8,128)S(1)} %copy-done.1, f32[2,8,3584]{2,1,0:T(8,128)S(1)} %collective-permute-done.4.refs_1_, f32[2,8,4608]{2,1,0:T(8,128)S(1)} %collective-permute-done.5.refs_2_, ...), custom_call_target="tpu_custom_call", output_to_operand_aliasing={{0}: (7, {})} | custom-call | flops 58982400 | bytes 7340032 | tf_op jit(solution)/shard_map/pallas_call | solution.py:134
  98.6 10.9 %shard_map.71 = (f32[2,32,32768]{2,1,0:T(8,128)}, f32[8,16,2048]{2,1,0:T(8,128)}, f32[8,16,2048]{2,1,0:T(8,128)}) custom-call(f32[2,32,32768]{2,1,0:T(8,128)S(1)} %copy-done.1, f32[2,8,3584]{2,1,0:T(8,128)S(1)} %collective-permute-done.refs_1_, ...), custom_call_target="tpu_custom_call", output_to_operand_aliasing={{0}: (7, {}), {1}: (8, {}), {2}: (9, {})} | custom-call | flops 58982400 | bytes 7340032 | tf_op jit(solution)/shard_map/pallas_call | solution.py:134
  109.5 2.9 all-to-all-done
  112.4 3.6 all-to-all-start.1
  117.4 25.1 %all-to-all-done.1 = f32[8,16,2048]{2,1,0:T(8,128)S(1)} async-done(((f32[8,16,2048]{2,1,0:T(8,128)}), f32[8,16,2048]{2,1,0:T(8,128)S(1)}, u32[]{:S(2)}, u32[]{:S(2)}) %all-to-all-start.1) | async-done | bytes 1048608 | tf_op jit(solution)/shard_map/all_to_all | solution.py:230
  142.5 3.7 %all-to-all-start.2 = ((f32[8,16,2048]{2,1,0:T(8,128)}), f32[8,16,2048]{2,1,0:T(8,128)S(1)}, u32[]{:S(2)}, u32[]{:S(2)}) async-start(f32[8,16,2048]{2,1,0:T(8,128)} %get-tuple-element.37), calls=%async_computation.2 | async-start | bytes 2097152 | tf_op jit(solution)/shard_map/all_to_all | solution.py:230
  165.2 2.6 convolution_multiply_fusion
  167.8 4.8 %all-to-all-done.2 = f32[8,16,2048]{2,1,0:T(8,128)S(1)} async-done(((f32[8,16,2048]{2,1,0:T(8,128)}), f32[8,16,2048]{2,1,0:T(8,128)S(1)}, u32[]{:S(2)}, u32[]{:S(2)}) %all-to-all-start.2) | async-done | bytes 1048608 | tf_op jit(solution)/shard_map/all_to_all | solution.py:230
  172.6 3.6 all-to-all-start.4
  193.2 2.6 convolution_multiply_fusion.6
  195.8 29.4 %all-to-all-done.4.source = f32[8,32,2048]{2,1,0:T(8,128)S(1)} async-done(((f32[8,32,2048]{2,1,0:T(8,128)}), f32[8,32,2048]{2,1,0:T(8,128)S(1)}, u32[]{:S(2)}, u32[]{:S(2)}) %all-to-all-start.4) | async-done | bytes 2097184 | tf_op jit(solution)/shard_map/all_to_all | solution.py:230
  226.6 4.3 %all-to-all-start.3 = ((f32[8,32,2048]{2,1,0:T(8,128)}), f32[8,32,2048]{2,1,0:T(8,128)}, u32[]{:S(2)}, u32[]{:S(2)}) async-start(f32[8,32,2048]{2,1,0:T(8,128)} %bitcast.112), calls=%async_computation.3 | async-start | bytes 4194304 | tf_op jit(solution)/shard_map/all_to_all | solution.py:230
  230.9 64.7 %shard_map.72.refs_0_ = f32[32,32768]{1,0:T(8,128)} custom-call(f32[8,32,2048]{2,1,0:T(8,128)} %copy-done.4), custom_call_target="tpu_custom_call" | custom-call | bytes 4194304 | tf_op jit(solution)/shard_map/pallas_call | solution.py:172
  295.7 64.7 %shard_map.73 = f32[32,32768]{1,0:T(8,128)} custom-call(f32[8,32,2048]{2,1,0:T(8,128)} %all-to-all-done.3.source, f32[32,32768]{1,0:T(8,128)} %shard_map.72.refs_0_), custom_call_target="tpu_custom_call", output_to_operand_aliasing={{}: (1, {})} | custom-call | bytes 4194304 | tf_op jit(solution)/shard_map/pallas_call | solution.py:172
  (81 shorter events, 54.3 us)
Async XLA Ops:
  2.8 24.9 %collective-permute-start.3 = (f32[19,4608]{1,0:T(8,128)S(1)}, f32[19,4608]{1,0:T(8,128)S(1)}, u32[]{:S(2)}, u32[]{:S(2)}) collective-permute-start(f32[19,4608]{1,0:T(8,128)S(1)} %pad_maximum_fusion.4), channel_id=1, source_target_pairs={{0,24},{8,0},{16,8},{24,16},{1,25},{9,1},{17,9},{25,17},{2,26},{10... | collective-permute-start | bytes 1050632 | tf_op jit(solution)/shard_map/ppermute | solution.py:30
  6.8 7.3 %copy-start.10 = (f32[32]{0:T(128)S(1)}, f32[32]{0:T(128)}, u32[]{:S(2)}) copy-start(f32[32]{0:T(128)} %param.8) | copy-start | bytes 388
  7.8 18.0 %collective-permute-start.2 = (f32[19,3584]{1,0:T(8,128)S(1)}, f32[19,3584]{1,0:T(8,128)}, u32[]{:S(2)}, u32[]{:S(2)}) collective-permute-start(f32[19,3584]{1,0:T(8,128)S(1)} %pad_maximum_fusion.5), channel_id=1, source_target_pairs={{0,8},{8,16},{16,24},{24,0},{1,9},{9,17},{17,25},{25,1},{2,10},{10... | collective-permute-start | bytes 817160 | tf_op jit(solution)/shard_map/ppermute | solution.py:30
  9.1 37.3 %collective-permute-start.7 = (f32[2,8,4608]{2,1,0:T(8,128)S(1)}, f32[2,8,4608]{2,1,0:T(8,128)S(1)}, u32[]{:S(2)}, u32[]{:S(2)}) collective-permute-start(f32[2,8,4608]{2,1,0:T(8,128)S(1)} %get-tuple-element.40), channel_id=1, source_target_pairs={{0,24},{8,0},{16,8},{24,16},{1,25},{9,1},{17,9},{25,17},{2,26},{10... | collective-permute-start | bytes 884744 | tf_op jit(solution)/shard_map/ppermute | solution.py:30
  14.1 32.3 %collective-permute-start.6 = (f32[2,8,3584]{2,1,0:T(8,128)}, f32[2,8,3584]{2,1,0:T(8,128)S(1)}, u32[]{:S(2)}, u32[]{:S(2)}) collective-permute-start(f32[2,8,3584]{2,1,0:T(8,128)} %get-tuple-element.43), channel_id=1, source_target_pairs={{0,8},{8,16},{16,24},{24,0},{1,9},{9,17},{17,25},{25,1},{2,10},{10... | collective-permute-start | bytes 688136 | tf_op jit(solution)/shard_map/ppermute | solution.py:30
  28.0 0.7 copy-start.7
  32.4 3.4 copy-start
  56.9 1.3 copy-start.2
  58.3 7.0 %copy-start.6 = (f32[2,8,3584]{2,1,0:T(8,128)S(1)}, f32[2,8,3584]{2,1,0:T(8,128)}, u32[]{:S(2)}) copy-start(f32[2,8,3584]{2,1,0:T(8,128)} %get-tuple-element.44) | copy-start | bytes 688132
  58.3 8.5 %copy-start.5 = (f32[2,8,3584]{2,1,0:T(8,128)S(1)}, f32[2,8,3584]{2,1,0:T(8,128)}, u32[]{:S(2)}) copy-start(f32[2,8,3584]{2,1,0:T(8,128)} %get-tuple-element.45) | copy-start | bytes 688132
  58.3 54.2 %all-to-all-start = ((f32[8,16,4096]{2,1,0:T(8,128)}), f32[8,16,4096]{2,1,0:T(8,128)}, u32[]{:S(2)}, u32[]{:S(2)}) async-start(f32[8,16,4096]{2,1,0:T(8,128)} %copy-done.2), calls=%async_computation | async-start | bytes 4194304 | tf_op jit(solution)/shard_map/all_to_all | solution.py:230
  63.3 21.0 %collective-permute-start.5 = (f32[2,8,4608]{2,1,0:T(8,128)S(1)}, f32[2,8,4608]{2,1,0:T(8,128)S(1)}, u32[]{:S(2)}, u32[]{:S(2)}) collective-permute-start(f32[2,8,4608]{2,1,0:T(8,128)S(1)} %get-tuple-element.41), channel_id=1, source_target_pairs={{0,24},{8,0},{16,8},{24,16},{1,25},{9,1},{17,9},{25,17},{2,26},{10... | collective-permute-start | bytes 884744 | tf_op jit(solution)/shard_map/ppermute | solution.py:30
  64.7 33.9 %collective-permute-start.1 = (f32[2,8,4608]{2,1,0:T(8,128)S(1)}, f32[2,8,4608]{2,1,0:T(8,128)S(1)}, u32[]{:S(2)}, u32[]{:S(2)}) collective-permute-start(f32[2,8,4608]{2,1,0:T(8,128)S(1)} %get-tuple-element.42), channel_id=1, source_target_pairs={{0,24},{8,0},{16,8},{24,16},{1,25},{9,1},{17,9},{25,17},{2,26},{10... | collective-permute-start | bytes 884744 | tf_op jit(solution)/shard_map/ppermute | solution.py:30
  65.2 19.0 %collective-permute-start.4 = (f32[2,8,3584]{2,1,0:T(8,128)S(1)}, f32[2,8,3584]{2,1,0:T(8,128)S(1)}, u32[]{:S(2)}, u32[]{:S(2)}) collective-permute-start(f32[2,8,3584]{2,1,0:T(8,128)S(1)} %copy-done.6), channel_id=1, source_target_pairs={{0,8},{8,16},{16,24},{24,0},{1,9},{9,17},{17,25},{25,1},{2,10},{10... | collective-permute-start | bytes 688136 | tf_op jit(solution)/shard_map/ppermute | solution.py:30
  66.7 31.8 %collective-permute-start = (f32[2,8,3584]{2,1,0:T(8,128)S(1)}, f32[2,8,3584]{2,1,0:T(8,128)S(1)}, u32[]{:S(2)}, u32[]{:S(2)}) collective-permute-start(f32[2,8,3584]{2,1,0:T(8,128)S(1)} %copy-done.5), channel_id=1, source_target_pairs={{0,8},{8,16},{16,24},{24,0},{1,9},{9,17},{17,25},{25,1},{2,10},{10... | collective-permute-start | bytes 688136 | tf_op jit(solution)/shard_map/ppermute | solution.py:30
  84.3 3.4 copy-start.1
  109.5 6.5 %copy-start.3 = (f32[256,256]{1,0:T(8,128)S(1)}, f32[256,256]{1,0:T(8,128)}, u32[]{:S(2)}) copy-start(f32[256,256]{1,0:T(8,128)} %param.10) | copy-start | bytes 786436
  112.4 30.1 %all-to-all-start.1 = ((f32[8,16,2048]{2,1,0:T(8,128)}), f32[8,16,2048]{2,1,0:T(8,128)S(1)}, u32[]{:S(2)}, u32[]{:S(2)}) async-start(f32[8,16,2048]{2,1,0:T(8,128)} %get-tuple-element.35), calls=%async_computation.1 | async-start | bytes 2097152 | tf_op jit(solution)/shard_map/all_to_all | solution.py:230
  142.5 30.1 %all-to-all-start.2 = ((f32[8,16,2048]{2,1,0:T(8,128)}), f32[8,16,2048]{2,1,0:T(8,128)S(1)}, u32[]{:S(2)}, u32[]{:S(2)}) async-start(f32[8,16,2048]{2,1,0:T(8,128)} %get-tuple-element.37), calls=%async_computation.2 | async-start | bytes 2097152 | tf_op jit(solution)/shard_map/all_to_all | solution.py:230
  146.3 2.2 copy-start.8
  172.6 52.6 %all-to-all-start.4 = ((f32[8,32,2048]{2,1,0:T(8,128)}), f32[8,32,2048]{2,1,0:T(8,128)S(1)}, u32[]{:S(2)}, u32[]{:S(2)}) async-start(f32[8,32,2048]{2,1,0:T(8,128)} %bitcast.111), calls=%async_computation.4 | async-start | bytes 4194304 | tf_op jit(solution)/shard_map/all_to_all | solution.py:230
  176.2 2.5 copy-start.9
  225.2 1.4 copy-start.4
  226.6 69.1 %all-to-all-start.3 = ((f32[8,32,2048]{2,1,0:T(8,128)}), f32[8,32,2048]{2,1,0:T(8,128)}, u32[]{:S(2)}, u32[]{:S(2)}) async-start(f32[8,32,2048]{2,1,0:T(8,128)} %bitcast.112), calls=%async_computation.3 | async-start | bytes 4194304 | tf_op jit(solution)/shard_map/all_to_all | solution.py:230

commit v2 on v0

--- a/solution.py
+++ b/solution.py
@@ -144,7 +144,7 @@
         compiler_params=pltpu.CompilerParams(vmem_limit_bytes=40 * 1024 * 1024),
         cost_estimate=pl.CostEstimate(
             flops=20 * TOTAL * GROUP * rows * COLS,
-            bytes_accessed=20 * GROUP * span,
+            bytes_accessed=28 * GROUP * span,
             transcendentals=0,
         ),
     )(*operands)
@@ -232,24 +232,28 @@
     halos = {0: (0, tuple(x[: 2 * GROUP].reshape(2, GROUP, -1) for x in (before, after)))}
     group = 1
     while group < groups:
-        count = 1 if group == 1 else groups - group
+        count = 1
         halo = neighbours(incident[:, group * GROUP : (group + count) * GROUP])
         for one in range(group, group + count):
             halos[one] = (group, halo)
         group += count
     detune = (jnp.cos(detuning)[:, None], jnp.sin(detuning)[:, None])
 
-    exit_field, (_, made) = sweep(
-        0, halos[0][1], 0, 1, dests, 1, incident, tables, detune, None, None
-    )
-    early = exchanged(made[0])
+    lead = max(groups // 2, 1)
+    exit_field = made = None
+    for group in range(lead):
+        first, halo = halos[group]
+        exit_field, made = sweep(
+            group, halo, first, 1, dests, lead, incident, tables, detune, exit_field, made
+        )
+    early = exchanged(made[1][0])
     late = []
-    if groups > 1:
+    if groups > lead:
         made = None
-        for group in range(1, groups):
+        for group in range(lead, groups):
             first, halo = halos[group]
             exit_field, made = sweep(
-                group, halo, first, halves, dests, groups - 1, incident, tables, detune, exit_field, made
+                group, halo, first, halves, dests, groups - lead, incident, tables, detune, exit_field, made
             )
         for half in range(halves):
             late.append(exchanged(made[1][half]))

time: 318 us -> 287 us (0.903)
  waiting for transfers between devices: 175 us -> 133 us
  local copies, waits for them, and re-layouts: 14.2 us -> 23.9 us
    all_to_all x5, waiting for transfers between devices: 129 us -> 106 us  [exchanged(): return lax.all_to_all(x, 'ang', split_axis=0, concat_axis=0, tiled=True)]
    ppermute x6 -> x8, waiting for transfers between devices: 45.6 us -> 27.6 us  [passed_along(): lax.ppermute(x, axis, [(i, (i + by) % devices) for i in range(devices)])]
    unnamed x19 -> x23, local copies, waits for them, and re-layouts: 7.86 us -> 13 us
    slice x4 -> x2, local copies, waits for them, and re-layouts: 0.01 us -> 3.62 us  [on_device(): early[:, :, half * part:(half + 1) * part]]
    ppermute x6 -> x8, starting transfers between devices: 8.66 us -> 11.9 us  [passed_along(): lax.ppermute(x, axis, [(i, (i + by) % devices) for i in range(devices)])]
  transfers between devices with their start and end apart: 11 -> 13, of which waited for: 7 -> 7; matrix products, arithmetic and copies ran while one was open for 13% -> 17% of each run, Pallas kernels for 12% -> 13%
where the time goes in v2:
time: 287 us; the launch traced here: 286 us
  waiting for transfers between devices  133 us (46%)
  Pallas kernels  54.3 us (19%)
  matrix products  34 us (12%)
  starting transfers between devices  32.2 us (11%)
  local copies, waits for them, and re-layouts  23.9 us (8%)
  other arithmetic  6.99 us (2%)
    all_to_all x5, waiting for transfers between devices, exchanged(): return lax.all_to_all(x, 'ang', split_axis=0, concat_axis=0, tiled=True)  106 us
    pallas_call x4, Pallas kernels, sweep(): pl.pallas_call(functools.partial(sweep_kernel, halves, dests), grid=(1,),...  43.1 us
    ppermute x8, waiting for transfers between devices, passed_along(): lax.ppermute(x, axis, [(i, (i + by) % devices) for i in range(devices)])  27.6 us
    all_to_all x5, starting transfers between devices, exchanged(): return lax.all_to_all(x, 'ang', split_axis=0, concat_axis=0, tiled=True)  20.3 us
    dot_general x12, matrix products, deconvolve(): lax.dot_general(backward, measured / blurred, (((0,), (0,)), ((), ())), p...  18 us
    dot_general x12, matrix products, deconvolve(): jnp.dot(response, estimate, precision=lax.Precision.HIGH, preferred_eleme...  15.9 us
    unnamed x23, local copies, waits for them, and re-layouts  13 us
    ppermute x8, starting transfers between devices, passed_along(): lax.ppermute(x, axis, [(i, (i + by) % devices) for i in range(devices)])  11.9 us
  transfers between devices with their start and end apart: 13, of which 7 were waited for; matrix products, arithmetic and copies ran while one was open for 17% of the time, Pallas kernels for 13%

profile of v2, /device:TPU:0, one launch (start us, length us, event | category | flops | bytes accessed | tf_op | source)
XLA Modules:
  0.0 285.6 jit_solution(10401328990598374489)
XLA Ops:
  2.8 3.9 %collective-permute-start.3 = (f32[19,4608]{1,0:T(8,128)S(1)}, f32[19,4608]{1,0:T(8,128)S(1)}, u32[]{:S(2)}, u32[]{:S(2)}) collective-permute-start(f32[19,4608]{1,0:T(8,128)S(1)} %pad_maximum_fusion.4), channel_id=1, source_target_pairs={{0,24},{8,0},{16,8},{24,16},{1,25},{9,1},{17,9},{25,17},{2,26},{10... | collective-permute-start | bytes 1050632 | tf_op jit(solution)/shard_map/ppermute | solution.py:30
  9.1 3.0 %collective-permute-start.7 = (f32[2,8,4608]{2,1,0:T(8,128)S(1)}, f32[2,8,4608]{2,1,0:T(8,128)S(1)}, u32[]{:S(2)}, u32[]{:S(2)}) collective-permute-start(f32[2,8,4608]{2,1,0:T(8,128)S(1)} %get-tuple-element.40), channel_id=1, source_target_pairs={{0,24},{8,0},{16,8},{24,16},{1,25},{9,1},{17,9},{25,17},{2,26},{10... | collective-permute-start | bytes 884744 | tf_op jit(solution)/shard_map/ppermute | solution.py:30
  14.3 11.5 %collective-permute-done.2 = f32[19,3584]{1,0:T(8,128)} collective-permute-done((f32[19,3584]{1,0:T(8,128)S(1)}, f32[19,3584]{1,0:T(8,128)}, u32[]{:S(2)}, u32[]{:S(2)}) %collective-permute-start.2) | collective-permute-done | bytes 272416 | tf_op jit(solution)/shard_map/ppermute | solution.py:30
  28.7 3.7 %sine_multiply_fusion = (f32[6,80,512]{2,1,0:T(8,128)S(1)}, f32[6,80,512]{2,1,0:T(8,128)S(1)}) fusion(f32[3,80,512]{2,1,0:T(8,128)S(1)} %get-tuple-element.53, f32[3,80,512]{2,1,0:T(8,128)S(1)} %get-tuple-element.52, f32[6]{0:T(128)S(1)} %copy-done.7), kind=kLoop, calls=%fused_computation.51 | loop fusion | flops 983040 | bytes 2949144 | tf_op jit(solution)/shard_map/mul | solution.py:179
  32.4 3.4 %copy-done = f32[2,32,32768]{2,1,0:T(8,128)S(1)} copy-done((f32[2,32,32768]{2,1,0:T(8,128)S(1)}, f32[2,32,32768]{2,1,0:T(8,128)}, u32[]{:S(2)}) %copy-start) | copy-done | bytes 8388632
  35.8 10.6 %shard_map.68 = (f32[2,32,32768]{2,1,0:T(8,128)}, f32[8,16,4096]{2,1,0:T(8,128)S(1)}) custom-call(f32[2,32,32768]{2,1,0:T(8,128)S(1)} %copy-done, f32[2,8,3584]{2,1,0:T(8,128)S(1)} %slice_bitcast_fusion.1.refs_1_, f32[2,8,4608]{2,1,0:T(8,128)S(1)} %slice_bitcast_fusion.refs_2_, f32[6,80,512]{2,1,0:T(8,128)S(1)} %get-tuple-element.51.refs_3_, ...), custom_call_target="tpu_custom_call" | custom-call | flops 58982400 | bytes 7340032 | tf_op jit(solution)/shard_map/pallas_call | solution.py:134
  46.4 10.6 %shard_map.69 = (f32[2,32,32768]{2,1,0:T(8,128)}, f32[8,16,4096]{2,1,0:T(8,128)S(1)}) custom-call(f32[2,32,32768]{2,1,0:T(8,128)S(1)} %copy-done, f32[2,8,3584]{2,1,0:T(8,128)S(1)} %collective-permute-done.6.refs_1_, f32[2,8,4608]{2,1,0:T(8,128)S(1)} %collective-permute-done.7.refs_2_, ...), custom_call_target="tpu_custom_call", output_to_operand_aliasing={{0}: (7, {}), {1}: (8, {})} | custom-call | flops 58982400 | bytes 7340032 | tf_op jit(solution)/shard_map/pallas_call | solution.py:134
  58.3 5.0 %all-to-all-start = ((f32[8,16,4096]{2,1,0:T(8,128)}), f32[8,16,4096]{2,1,0:T(8,128)}, u32[]{:S(2)}, u32[]{:S(2)}) async-start(f32[8,16,4096]{2,1,0:T(8,128)} %copy-done.2), calls=%async_computation | async-start | bytes 4194304 | tf_op jit(solution)/shard_map/all_to_all | solution.py:220
  68.2 16.0 %collective-permute-done.4.refs_1_ = f32[2,8,3584]{2,1,0:T(8,128)S(1)} collective-permute-done((f32[2,8,3584]{2,1,0:T(8,128)S(1)}, f32[2,8,3584]{2,1,0:T(8,128)S(1)}, u32[]{:S(2)}, u32[]{:S(2)}) %collective-permute-start.4) | collective-permute-done | bytes 229408 | tf_op jit(solution)/shard_map/ppermute | solution.py:30
  84.3 3.4 %copy-done.1 = f32[2,32,32768]{2,1,0:T(8,128)S(1)} copy-done((f32[2,32,32768]{2,1,0:T(8,128)S(1)}, f32[2,32,32768]{2,1,0:T(8,128)}, u32[]{:S(2)}) %copy-start.1) | copy-done | bytes 8388632
  87.6 10.9 %shard_map.70 = (f32[2,32,32768]{2,1,0:T(8,128)}, f32[8,16,2048]{2,1,0:T(8,128)}, f32[8,16,2048]{2,1,0:T(8,128)}) custom-call(f32[2,32,32768]{2,1,0:T(8,128)S(1)} %copy-done.1, f32[2,8,3584]{2,1,0:T(8,128)S(1)} %collective-permute-done.4.refs_1_, f32[2,8,4608]{2,1,0:T(8,128)S(1)} %collective-permute-done.5.refs_2_, ...), custom_call_target="tpu_custom_call", output_to_operand_aliasing={{0}: (7, {})} | custom-call | flops 58982400 | bytes 7340032 | tf_op jit(solution)/shard_map/pallas_call | solution.py:134
  98.6 10.9 %shard_map.71 = (f32[2,32,32768]{2,1,0:T(8,128)}, f32[8,16,2048]{2,1,0:T(8,128)}, f32[8,16,2048]{2,1,0:T(8,128)}) custom-call(f32[2,32,32768]{2,1,0:T(8,128)S(1)} %copy-done.1, f32[2,8,3584]{2,1,0:T(8,128)S(1)} %collective-permute-done.refs_1_, ...), custom_call_target="tpu_custom_call", output_to_operand_aliasing={{0}: (7, {}), {1}: (8, {}), {2}: (9, {})} | custom-call | flops 58982400 | bytes 7340032 | tf_op jit(solution)/shard_map/pallas_call | solution.py:134
  109.5 2.9 %all-to-all-done = f32[8,16,4096]{2,1,0:T(8,128)} async-done(((f32[8,16,4096]{2,1,0:T(8,128)}), f32[8,16,4096]{2,1,0:T(8,128)}, u32[]{:S(2)}, u32[]{:S(2)}) %all-to-all-start) | async-done | bytes 2097184 | tf_op jit(solution)/shard_map/all_to_all | solution.py:220
  112.4 3.6 %all-to-all-start.1 = ((f32[8,16,2048]{2,1,0:T(8,128)}), f32[8,16,2048]{2,1,0:T(8,128)S(1)}, u32[]{:S(2)}, u32[]{:S(2)}) async-start(f32[8,16,2048]{2,1,0:T(8,128)} %get-tuple-element.35), calls=%async_computation.1 | async-start | bytes 2097152 | tf_op jit(solution)/shard_map/all_to_all | solution.py:220
  117.4 25.1 %all-to-all-done.1 = f32[8,16,2048]{2,1,0:T(8,128)S(1)} async-done(((f32[8,16,2048]{2,1,0:T(8,128)}), f32[8,16,2048]{2,1,0:T(8,128)S(1)}, u32[]{:S(2)}, u32[]{:S(2)}) %all-to-all-start.1) | async-done | bytes 1048608 | tf_op jit(solution)/shard_map/all_to_all | solution.py:220
  142.5 3.7 %all-to-all-start.2 = ((f32[8,16,2048]{2,1,0:T(8,128)}), f32[8,16,2048]{2,1,0:T(8,128)S(1)}, u32[]{:S(2)}, u32[]{:S(2)}) async-start(f32[8,16,2048]{2,1,0:T(8,128)} %get-tuple-element.37), calls=%async_computation.2 | async-start | bytes 2097152 | tf_op jit(solution)/shard_map/all_to_all | solution.py:220
  167.8 4.8 %all-to-all-done.2 = f32[8,16,2048]{2,1,0:T(8,128)S(1)} async-done(((f32[8,16,2048]{2,1,0:T(8,128)}), f32[8,16,2048]{2,1,0:T(8,128)S(1)}, u32[]{:S(2)}, u32[]{:S(2)}) %all-to-all-start.2) | async-done | bytes 1048608 | tf_op jit(solution)/shard_map/all_to_all | solution.py:220
  172.6 3.6 %all-to-all-start.4 = ((f32[8,32,2048]{2,1,0:T(8,128)}), f32[8,32,2048]{2,1,0:T(8,128)S(1)}, u32[]{:S(2)}, u32[]{:S(2)}) async-start(f32[8,32,2048]{2,1,0:T(8,128)} %bitcast.111), calls=%async_computation.4 | async-start | bytes 4194304 | tf_op jit(solution)/shard_map/all_to_all | solution.py:220
  193.2 2.6 convolution_multiply_fusion.6
  195.8 29.4 %all-to-all-done.4.source = f32[8,32,2048]{2,1,0:T(8,128)S(1)} async-done(((f32[8,32,2048]{2,1,0:T(8,128)}), f32[8,32,2048]{2,1,0:T(8,128)S(1)}, u32[]{:S(2)}, u32[]{:S(2)}) %all-to-all-start.4) | async-done | bytes 2097184 | tf_op jit(solution)/shard_map/all_to_all | solution.py:220
  226.6 4.3 %all-to-all-start.3 = ((f32[8,32,2048]{2,1,0:T(8,128)}), f32[8,32,2048]{2,1,0:T(8,128)}, u32[]{:S(2)}, u32[]{:S(2)}) async-start(f32[8,32,2048]{2,1,0:T(8,128)} %bitcast.112), calls=%async_computation.3 | async-start | bytes 4194304 | tf_op jit(solution)/shard_map/all_to_all | solution.py:220
  230.9 5.6 %shard_map.72.refs_0_ = f32[32,32768]{1,0:T(8,128)} custom-call(f32[8,32,2048]{2,1,0:T(8,128)} %copy-done.4), custom_call_target="tpu_custom_call" | custom-call | bytes 4194304 | tf_op jit(solution)/shard_map/pallas_call | solution.py:161
  236.6 43.4 %all-to-all-done.3.source = f32[8,32,2048]{2,1,0:T(8,128)} async-done(((f32[8,32,2048]{2,1,0:T(8,128)}), f32[8,32,2048]{2,1,0:T(8,128)}, u32[]{:S(2)}, u32[]{:S(2)}) %all-to-all-start.3) | async-done | bytes 2097184 | tf_op jit(solution)/shard_map/all_to_all | solution.py:220
  280.0 5.6 %shard_map.73 = f32[32,32768]{1,0:T(8,128)} custom-call(f32[8,32,2048]{2,1,0:T(8,128)} %all-to-all-done.3.source, f32[32,32768]{1,0:T(8,128)} %shard_map.72.refs_0_), custom_call_target="tpu_custom_call", output_to_operand_aliasing={{}: (1, {})} | custom-call | bytes 4194304 | tf_op jit(solution)/shard_map/pallas_call | solution.py:161
  (81 shorter events, 56.9 us)
Async XLA Ops:
  2.8 24.9 %collective-permute-start.3 = (f32[19,4608]{1,0:T(8,128)S(1)}, f32[19,4608]{1,0:T(8,128)S(1)}, u32[]{:S(2)}, u32[]{:S(2)}) collective-permute-start(f32[19,4608]{1,0:T(8,128)S(1)} %pad_maximum_fusion.4), channel_id=1, source_target_pairs={{0,24},{8,0},{16,8},{24,16},{1,25},{9,1},{17,9},{25,17},{2,26},{10... | collective-permute-start | bytes 1050632 | tf_op jit(solution)/shard_map/ppermute | solution.py:30
  6.8 7.3 %copy-start.10 = (f32[32]{0:T(128)S(1)}, f32[32]{0:T(128)}, u32[]{:S(2)}) copy-start(f32[32]{0:T(128)} %param.8) | copy-start | bytes 388
  7.8 18.0 %collective-permute-start.2 = (f32[19,3584]{1,0:T(8,128)S(1)}, f32[19,3584]{1,0:T(8,128)}, u32[]{:S(2)}, u32[]{:S(2)}) collective-permute-start(f32[19,3584]{1,0:T(8,128)S(1)} %pad_maximum_fusion.5), channel_id=1, source_target_pairs={{0,8},{8,16},{16,24},{24,0},{1,9},{9,17},{17,25},{25,1},{2,10},{10... | collective-permute-start | bytes 817160 | tf_op jit(solution)/shard_map/ppermute | solution.py:30
  9.1 37.3 %collective-permute-start.7 = (f32[2,8,4608]{2,1,0:T(8,128)S(1)}, f32[2,8,4608]{2,1,0:T(8,128)S(1)}, u32[]{:S(2)}, u32[]{:S(2)}) collective-permute-start(f32[2,8,4608]{2,1,0:T(8,128)S(1)} %get-tuple-element.40), channel_id=1, source_target_pairs={{0,24},{8,0},{16,8},{24,16},{1,25},{9,1},{17,9},{25,17},{2,26},{10... | collective-permute-start | bytes 884744 | tf_op jit(solution)/shard_map/ppermute | solution.py:30
  14.1 32.3 %collective-permute-start.6 = (f32[2,8,3584]{2,1,0:T(8,128)}, f32[2,8,3584]{2,1,0:T(8,128)S(1)}, u32[]{:S(2)}, u32[]{:S(2)}) collective-permute-start(f32[2,8,3584]{2,1,0:T(8,128)} %get-tuple-element.43), channel_id=1, source_target_pairs={{0,8},{8,16},{16,24},{24,0},{1,9},{9,17},{17,25},{25,1},{2,10},{10... | collective-permute-start | bytes 688136 | tf_op jit(solution)/shard_map/ppermute | solution.py:30
  28.0 0.7 copy-start.7
  32.4 3.4 %copy-start = (f32[2,32,32768]{2,1,0:T(8,128)S(1)}, f32[2,32,32768]{2,1,0:T(8,128)}, u32[]{:S(2)}) copy-start(f32[2,32,32768]{2,1,0:T(8,128)} %refs_0_.7) | copy-start | bytes 25165828
  56.9 1.3 copy-start.2
  58.3 7.0 %copy-start.6 = (f32[2,8,3584]{2,1,0:T(8,128)S(1)}, f32[2,8,3584]{2,1,0:T(8,128)}, u32[]{:S(2)}) copy-start(f32[2,8,3584]{2,1,0:T(8,128)} %get-tuple-element.44) | copy-start | bytes 688132
  58.3 8.5 %copy-start.5 = (f32[2,8,3584]{2,1,0:T(8,128)S(1)}, f32[2,8,3584]{2,1,0:T(8,128)}, u32[]{:S(2)}) copy-start(f32[2,8,3584]{2,1,0:T(8,128)} %get-tuple-element.45) | copy-start | bytes 688132
  58.3 54.2 %all-to-all-start = ((f32[8,16,4096]{2,1,0:T(8,128)}), f32[8,16,4096]{2,1,0:T(8,128)}, u32[]{:S(2)}, u32[]{:S(2)}) async-start(f32[8,16,4096]{2,1,0:T(8,128)} %copy-done.2), calls=%async_computation | async-start | bytes 4194304 | tf_op jit(solution)/shard_map/all_to_all | solution.py:220
  63.3 21.0 %collective-permute-start.5 = (f32[2,8,4608]{2,1,0:T(8,128)S(1)}, f32[2,8,4608]{2,1,0:T(8,128)S(1)}, u32[]{:S(2)}, u32[]{:S(2)}) collective-permute-start(f32[2,8,4608]{2,1,0:T(8,128)S(1)} %get-tuple-element.41), channel_id=1, source_target_pairs={{0,24},{8,0},{16,8},{24,16},{1,25},{9,1},{17,9},{25,17},{2,26},{10... | collective-permute-start | bytes 884744 | tf_op jit(solution)/shard_map/ppermute | solution.py:30
  64.7 33.9 %collective-permute-start.1 = (f32[2,8,4608]{2,1,0:T(8,128)S(1)}, f32[2,8,4608]{2,1,0:T(8,128)S(1)}, u32[]{:S(2)}, u32[]{:S(2)}) collective-permute-start(f32[2,8,4608]{2,1,0:T(8,128)S(1)} %get-tuple-element.42), channel_id=1, source_target_pairs={{0,24},{8,0},{16,8},{24,16},{1,25},{9,1},{17,9},{25,17},{2,26},{10... | collective-permute-start | bytes 884744 | tf_op jit(solution)/shard_map/ppermute | solution.py:30
  65.2 19.0 %collective-permute-start.4 = (f32[2,8,3584]{2,1,0:T(8,128)S(1)}, f32[2,8,3584]{2,1,0:T(8,128)S(1)}, u32[]{:S(2)}, u32[]{:S(2)}) collective-permute-start(f32[2,8,3584]{2,1,0:T(8,128)S(1)} %copy-done.6), channel_id=1, source_target_pairs={{0,8},{8,16},{16,24},{24,0},{1,9},{9,17},{17,25},{25,1},{2,10},{10... | collective-permute-start | bytes 688136 | tf_op jit(solution)/shard_map/ppermute | solution.py:30
  66.7 31.8 %collective-permute-start = (f32[2,8,3584]{2,1,0:T(8,128)S(1)}, f32[2,8,3584]{2,1,0:T(8,128)S(1)}, u32[]{:S(2)}, u32[]{:S(2)}) collective-permute-start(f32[2,8,3584]{2,1,0:T(8,128)S(1)} %copy-done.5), channel_id=1, source_target_pairs={{0,8},{8,16},{16,24},{24,0},{1,9},{9,17},{17,25},{25,1},{2,10},{10... | collective-permute-start | bytes 688136 | tf_op jit(solution)/shard_map/ppermute | solution.py:30
  84.3 3.4 %copy-start.1 = (f32[2,32,32768]{2,1,0:T(8,128)S(1)}, f32[2,32,32768]{2,1,0:T(8,128)}, u32[]{:S(2)}) copy-start(f32[2,32,32768]{2,1,0:T(8,128)} %refs_0_.7) | copy-start | bytes 25165828
  109.5 6.5 %copy-start.3 = (f32[256,256]{1,0:T(8,128)S(1)}, f32[256,256]{1,0:T(8,128)}, u32[]{:S(2)}) copy-start(f32[256,256]{1,0:T(8,128)} %param.10) | copy-start | bytes 786436
  112.4 30.1 %all-to-all-start.1 = ((f32[8,16,2048]{2,1,0:T(8,128)}), f32[8,16,2048]{2,1,0:T(8,128)S(1)}, u32[]{:S(2)}, u32[]{:S(2)}) async-start(f32[8,16,2048]{2,1,0:T(8,128)} %get-tuple-element.35), calls=%async_computation.1 | async-start | bytes 2097152 | tf_op jit(solution)/shard_map/all_to_all | solution.py:220
  142.5 30.1 %all-to-all-start.2 = ((f32[8,16,2048]{2,1,0:T(8,128)}), f32[8,16,2048]{2,1,0:T(8,128)S(1)}, u32[]{:S(2)}, u32[]{:S(2)}) async-start(f32[8,16,2048]{2,1,0:T(8,128)} %get-tuple-element.37), calls=%async_computation.2 | async-start | bytes 2097152 | tf_op jit(solution)/shard_map/all_to_all | solution.py:220
  146.3 2.2 copy-start.8
  172.6 52.6 %all-to-all-start.4 = ((f32[8,32,2048]{2,1,0:T(8,128)}), f32[8,32,2048]{2,1,0:T(8,128)S(1)}, u32[]{:S(2)}, u32[]{:S(2)}) async-start(f32[8,32,2048]{2,1,0:T(8,128)} %bitcast.111), calls=%async_computation.4 | async-start | bytes 4194304 | tf_op jit(solution)/shard_map/all_to_all | solution.py:220
  176.2 2.5 copy-start.9
  225.2 1.4 copy-start.4
  226.6 53.4 %all-to-all-start.3 = ((f32[8,32,2048]{2,1,0:T(8,128)}), f32[8,32,2048]{2,1,0:T(8,128)}, u32[]{:S(2)}, u32[]{:S(2)}) async-start(f32[8,32,2048]{2,1,0:T(8,128)} %bitcast.112), calls=%async_computation.3 | async-start | bytes 4194304 | tf_op jit(solution)/shard_map/all_to_all | solution.py:220
